TPU v7x, 32 devices: a whole 2x2x4 slice. The times are simulated.
32 devices in a mesh: lon: 4 (over x, core), lat: 2 (over y), head: 4 (over z).
Axes of the slice: x: 2, y: 2, z: 4, core: 2. Of those that a mesh axis runs over, the one named last changes fastest.
Arguments:
- tokens: bfloat16 [48, 48, 4, 512], P('lon', 'lat', None, 'head'), may hold values from -6 to 6
- qkv_weight: bfloat16 [2, 3, 512, 512], P(None, None, None, 'head')
- out_weight: bfloat16 [2, 512, 512], P(None, 'head'), may hold values from -0.25 to 0.25
- up_weight: bfloat16 [2, 512, 2048], P(None, None, 'head'), may hold values from -0.25 to 0.25
- down_weight: bfloat16 [2, 2048, 512], P(None, 'head'), may hold values from -0.125 to 0.125
- bias_table: float32 [2, 759, 8], P(None, None, 'head'), may hold values from -4 to 4
- bias_index: int32 [144, 144], replicated, may hold values from 0 to 758
- regions: int32 [48, 48, 4], P('lon', 'lat'), may hold values from 0 to 7, as said below
Outputs:
- state: bfloat16 [48, 48, 4, 512], P('lon', 'lat', None, 'head')
Inputs may be any that keep to these rules, and one draw needn't show every extreme that they name: regions is a class id (0 to 3): 2 if the latitude row is among the first 3, plus 1 if the level is 0.
All inputs are finite; a program needn't handle non-finite values.
Results may differ from a plain program's by a relative error of at most 0.02.
Values may be sent and summed in bfloat16 or wider, within the bound.
A program may use at most 64 MiB of HBM per device.

v0:
```python
import jax
import jax.numpy as jnp
from jax import lax
from jax.sharding import PartitionSpec as P

WIN_LON = 12
WIN_LAT = 6
WIN_LEV = 2


EPS = 1e-05
MASKED = -1000000000.0


def passed_along(shard, axis, by):
    size = lax.axis_size(axis)
    return lax.ppermute(shard, axis, [(i, (i + by) % size) for i in range(size)])


def layer_norm(values):
    values = values.astype(jnp.float32)
    center = values - jnp.mean(values, axis=-1, keepdims=True)
    spread = jnp.mean(center * center, axis=-1, keepdims=True)
    return (center * lax.rsqrt(spread + EPS)).astype(jnp.bfloat16)


def split_windows(arr):
    lon_n, lat_n, lev_n, cols = arr.shape
    arr = arr.reshape(
        lon_n // WIN_LON, WIN_LON, lat_n // WIN_LAT, WIN_LAT, lev_n // WIN_LEV, WIN_LEV, cols
    )
    arr = arr.transpose(0, 2, 4, 1, 3, 5, 6)
    return arr.reshape(-1, WIN_LON * WIN_LAT * WIN_LEV, cols)


def join_windows(arr, lon_n, lat_n, lev_n):
    cols = arr.shape[-1]
    arr = arr.reshape(
        lon_n // WIN_LON, lat_n // WIN_LAT, lev_n // WIN_LEV, WIN_LON, WIN_LAT, WIN_LEV, cols
    )
    arr = arr.transpose(0, 3, 1, 4, 2, 5, 6)
    return arr.reshape(lon_n, lat_n, lev_n, cols)


def attend(normed, weight, table, index, marks):
    lon_n, lat_n, lev_n, width = normed.shape
    heads = table.shape[1]
    cols = weight.shape[2]
    head_dim = cols // heads
    merged = jnp.einsum(
        "lavd,tdc->tlavc", normed, weight, preferred_element_type=jnp.float32
    ).astype(jnp.bfloat16)
    query = split_windows(merged[0])
    count = query.shape[0]
    query = query.reshape(count, -1, heads, head_dim)
    keys = split_windows(merged[1]).reshape(count, -1, heads, head_dim)
    values = split_windows(merged[2]).reshape(count, -1, heads, head_dim)
    bias = jnp.take(table, index, axis=0).transpose(2, 0, 1)
    scores = jnp.einsum("wqhe,wkhe->whqk", query, keys, preferred_element_type=jnp.float32)
    scores = scores * head_dim ** (-0.5) + bias[None]
    if marks is not None:
        flat = split_windows(marks[..., None])[..., 0]
        same = flat[:, :, None] == flat[:, None, :]
        scores = jnp.where(same[:, None], scores, MASKED)
    scores = scores - jnp.max(scores, axis=-1, keepdims=True)
    expo = jnp.exp(scores)
    probs = (expo / jnp.sum(expo, axis=-1, keepdims=True)).astype(jnp.bfloat16)
    out = jnp.einsum("whqk,wkhe->wqhe", probs, values, preferred_element_type=jnp.float32).astype(
        jnp.bfloat16
    )
    return join_windows(out.reshape(count, -1, cols), lon_n, lat_n, lev_n)


def roll_forward(field, marks):
    lon_half = WIN_LON // 2
    lat_half = WIN_LAT // 2
    got_field, got_marks = passed_along((field[:lon_half], marks[:lon_half]), "lon", -1)
    field = jnp.concatenate([field[lon_half:], got_field], axis=0)
    marks = jnp.concatenate([marks[lon_half:], got_marks], axis=0)
    got_field, got_marks = passed_along((field[:, :lat_half], marks[:, :lat_half]), "lat", -1)
    field = jnp.concatenate([field[:, lat_half:], got_field], axis=1)
    marks = jnp.concatenate([marks[:, lat_half:], got_marks], axis=1)
    return (jnp.roll(field, -1, axis=2), jnp.roll(marks, -1, axis=2))


def roll_back(mixed):
    lon_half = WIN_LON // 2
    lat_half = WIN_LAT // 2
    mixed = jnp.roll(mixed, 1, axis=2)
    got = passed_along(mixed[:, -lat_half:], "lat", 1)
    mixed = jnp.concatenate([got, mixed[:, :-lat_half]], axis=1)
    got = passed_along(mixed[-lon_half:], "lon", 1)
    return jnp.concatenate([got, mixed[:-lon_half]], axis=0)


def head_features(state, whole):
    whole = lax.all_gather(state, "head", axis=3, tiled=True)
    return whole


def local(tokens, qkv_weight, out_weight, up_weight, down_weight, bias_table, bias_index, regions):
    state = tokens
    whole = None
    region_marks = regions.astype(jnp.bfloat16)
    for block in range(2):
        marks = None
        if block == 1:
            whole = head_features(state, whole)
            normed, marks = roll_forward(layer_norm(whole), region_marks)
        else:
            whole = head_features(state, whole)
            normed = layer_norm(whole)
        mixed = attend(normed, qkv_weight[block], bias_table[block], bias_index, marks)
        if block == 1:
            mixed = roll_back(mixed)
        term = jnp.einsum(
            "lavc,cd->lavd", mixed, out_weight[block], preferred_element_type=jnp.float32
        )
        part = lax.psum_scatter(
            term.astype(jnp.bfloat16), "head", scatter_dimension=3, tiled=True
        ).astype(jnp.float32)
        state = (state.astype(jnp.float32) + part).astype(jnp.bfloat16)
        whole = lax.all_gather(state, "head", axis=3, tiled=True)
        normed = layer_norm(whole)
        hidden = jax.nn.gelu(
            jnp.einsum(
                "lavd,df->lavf", normed, up_weight[block], preferred_element_type=jnp.float32
            )
        ).astype(jnp.bfloat16)
        term = jnp.einsum(
            "lavf,fd->lavd", hidden, down_weight[block], preferred_element_type=jnp.float32
        )
        part = lax.psum_scatter(
            term.astype(jnp.bfloat16), "head", scatter_dimension=3, tiled=True
        ).astype(jnp.float32)
        state = (state.astype(jnp.float32) + part).astype(jnp.bfloat16)
        whole = None
    return state


def solution(mesh):
    return jax.shard_map(
        local,
        mesh=mesh,
        in_specs=(
            P("lon", "lat", None, "head"),
            P(None, None, None, "head"),
            P(None, "head", None),
            P(None, None, "head"),
            P(None, "head", None),
            P(None, None, "head"),
            P(),
            P("lon", "lat", None),
        ),
        out_specs=P("lon", "lat", None, "head"),
        check_vma=False,
    )
```

profile of v0, /device:TPU:0, one launch (start us, length us, event | category | flops | bytes accessed | tf_op | source)
XLA Modules:
  0.0 507.3 jit_solution(13748681438842024388)
XLA Ops:
  6.5 0.7 all-gather.5.cloned.1.call-update
  7.3 0.7 fusion.151
  8.2 0.9 compare_select_fusion
  9.3 38.8 %gather_fusion = f32[20736,2]{1,0:T(8,128)} fusion(f32[759,2]{1,0:T(8,128)S(1)} %bitcast.122, s32[21504]{0:T(1024)S(1)} %pad_clamp_fusion), kind=kCustom, calls=%fused_computation.clone | custom fusion | bytes 414720 | tf_op jit(solution)/shard_map/jit(_take)/gather | solution.py:58
  48.1 8.3 %copy.186 = f32[144,144,2]{0,1,2:T(8,128)S(1)} copy(f32[144,144,2]{2,1,0:T(8,128)} %bitcast.125) | data formatting | bytes 331776 | tf_op jit(solution)/shard_map/jit(_take)/gather | solution.py:58
  56.8 38.8 %gather_fusion.1 = f32[20736,2]{1,0:T(8,128)} fusion(f32[759,2]{1,0:T(8,128)S(1)} %bitcast.123, s32[21504]{0:T(1024)S(1)} %pad_clamp_fusion), kind=kCustom, calls=%fused_computation.1.clone | custom fusion | bytes 414720 | tf_op jit(solution)/shard_map/jit(_take)/gather | solution.py:58
  95.6 8.3 %copy.206 = f32[144,144,2]{0,1,2:T(8,128)S(1)} copy(f32[144,144,2]{2,1,0:T(8,128)} %bitcast.124) | data formatting | bytes 331776 | tf_op jit(solution)/shard_map/jit(_take)/gather | solution.py:58
  104.0 1.9 convert_reduce_fusion.3
  106.0 1.2 fusion.10
  107.2 0.9 fusion.46
  108.1 0.8 fusion.36
  110.9 2.4 fusion.153
  113.2 2.1 fusion.38
  115.3 0.5 copy.189
  116.3 0.5 convolution_convert_fusion.3
  116.8 8.0 %copy.228 = bf16[12,24,4,512]{1,2,0,3:T(4,128)(2,1)} copy(bf16[12,24,4,512]{3,1,2,0:T(8,128)(2,1)S(1)} %convolution_convert_fusion.3) | data formatting | bytes 2359296
  124.8 14.7 %reshape.108 = bf16[512,1152]{1,0:T(8,128)(2,1)} reshape(bf16[512,12,4,24]{3,2,1,0:T(4,128)(2,1)} %bitcast.126) | data formatting | bytes 2359296
  139.8 31.9 %reduce-scatter.13.cloned.1.call-done = bf16[128,1152]{1,0:T(8,128)(2,1)} async-done(((bf16[512,1152]{1,0:T(8,128)(2,1)}), bf16[128,1152]{1,0:T(8,128)(2,1)}) %reduce-scatter.13.cloned.1.call-update) | async-done | bytes 294928
  171.6 5.3 %reshape.109 = bf16[128,12,4,24]{3,2,1,0:T(4,128)(2,1)S(1)} reshape(bf16[128,1152]{1,0:T(8,128)(2,1)} %reduce-scatter.13.cloned.1.call-done) | data formatting | bytes 589824
  176.9 1.4 copy.229
  178.3 0.8 add_convert_fusion.3
  179.2 30.6 %all-gather.7.cloned.1.call-done = bf16[12,24,4,512]{3,1,2,0:T(8,128)(2,1)} async-done(((bf16[12,24,4,128]{3,1,2,0:T(8,128)(2,1)}), bf16[12,24,4,512]{3,1,2,0:T(8,128)(2,1)}) %all-gather.7.cloned.1.call-update) | async-done | bytes 1179664 | tf_op jit(solution)/shard_map/all_gather | solution.py:123
  209.7 1.6 convert_reduce_fusion.2
  211.4 1.8 fusion.16
  213.2 3.2 convolution_convert_fusion.2
  216.4 8.0 %copy.230 = bf16[12,24,4,512]{1,2,0,3:T(4,128)(2,1)} copy(bf16[12,24,4,512]{3,1,2,0:T(8,128)(2,1)S(1)} %convolution_convert_fusion.2) | data formatting | bytes 2359296
  224.3 14.7 %reshape.110 = bf16[512,1152]{1,0:T(8,128)(2,1)} reshape(bf16[512,12,4,24]{3,2,1,0:T(4,128)(2,1)} %bitcast.127) | data formatting | bytes 2359296
  239.2 27.6 %reduce-scatter.15.cloned.1.call-done = bf16[128,1152]{1,0:T(8,128)(2,1)} async-done(((bf16[512,1152]{1,0:T(8,128)(2,1)}), bf16[128,1152]{1,0:T(8,128)(2,1)}) %reduce-scatter.15.cloned.1.call-update) | async-done | bytes 294928
  266.8 5.3 %reshape.111 = bf16[128,12,4,24]{3,2,1,0:T(4,128)(2,1)S(1)} reshape(bf16[128,1152]{1,0:T(8,128)(2,1)} %reduce-scatter.15.cloned.1.call-done) | data formatting | bytes 589824
  272.0 1.4 copy.231
  273.4 0.8 add_convert_fusion.2
  274.5 30.4 %all-gather.9.cloned.1.call-done = bf16[12,24,4,512]{3,1,2,0:T(8,128)(2,1)} async-done(((bf16[12,24,4,128]{3,1,2,0:T(8,128)(2,1)}), bf16[12,24,4,512]{3,1,2,0:T(8,128)(2,1)}) %all-gather.9.cloned.1.call-update) | async-done | bytes 1179664 | tf_op jit(solution)/shard_map/all_gather | solution.py:97
  304.9 1.6 convert_reduce_fusion.1
  306.5 1.8 fusion.14
  308.8 0.7 collective-permute-start
  310.0 7.0 %collective-permute-done.2 = bf16[6,24,4]{1,2,0:T(4,128)(2,1)S(1)} collective-permute-done((bf16[6,24,4]{1,2,0:T(4,128)(2,1)S(1)}, bf16[6,24,4]{1,2,0:T(4,128)(2,1)S(1)}, u32[]{:S(2)}, u32[]{:S(2)}) %collective-permute-start.2) | collective-permute-done | bytes 1184 | tf_op jit(solution)/shard_map/ppermute | solution.py:17
  317.0 1.5 collective-permute-start.3
  318.6 2.1 collective-permute-done.3
  321.1 0.5 copy.236
  321.9 1.5 collective-permute-start.1
  324.0 4.2 collective-permute-done.1
  328.4 0.8 fusion.37
  331.2 2.5 fusion.158
  333.7 2.1 fusion.39
  335.8 0.5 copy.209
  337.1 1.8 collective-permute-start.4
  338.9 2.4 collective-permute-done.4
  341.4 4.6 collective-permute-done.5
  346.4 8.0 %copy.232 = bf16[12,24,4,512]{1,2,0,3:T(4,128)(2,1)} copy(bf16[12,24,4,512]{3,1,2,0:T(8,128)(2,1)S(1)} %convolution_convert_fusion.1) | data formatting | bytes 2359296
  354.4 14.7 %reshape.112 = bf16[512,1152]{1,0:T(8,128)(2,1)} reshape(bf16[512,12,4,24]{3,2,1,0:T(4,128)(2,1)} %bitcast.128) | data formatting | bytes 2359296
  369.5 27.9 %reduce-scatter.17.cloned.1.call-done = bf16[128,1152]{1,0:T(8,128)(2,1)} async-done(((bf16[512,1152]{1,0:T(8,128)(2,1)}), bf16[128,1152]{1,0:T(8,128)(2,1)}) %reduce-scatter.17.cloned.1.call-update) | async-done | bytes 294928
  397.3 5.3 %reshape.113 = bf16[128,12,4,24]{3,2,1,0:T(4,128)(2,1)S(1)} reshape(bf16[128,1152]{1,0:T(8,128)(2,1)} %reduce-scatter.17.cloned.1.call-done) | data formatting | bytes 589824
  402.6 1.4 copy.233
  404.0 0.8 add_convert_fusion.1
  404.9 30.6 %all-gather.11.cloned.1.call-done = bf16[12,24,4,512]{3,1,2,0:T(8,128)(2,1)} async-done(((bf16[12,24,4,128]{3,1,2,0:T(8,128)(2,1)}), bf16[12,24,4,512]{3,1,2,0:T(8,128)(2,1)}) %all-gather.11.cloned.1.call-update) | async-done | bytes 1179664 | tf_op jit(solution)/shard_map/all_gather | solution.py:123
  435.5 1.6 convert_reduce_fusion
  437.1 1.8 fusion.12
  438.9 3.0 convolution_convert_fusion
  442.0 8.0 %copy.234 = bf16[12,24,4,512]{1,2,0,3:T(4,128)(2,1)} copy(bf16[12,24,4,512]{3,1,2,0:T(8,128)(2,1)S(1)} %convolution_convert_fusion) | data formatting | bytes 2359296
  449.9 14.7 %reshape.114 = bf16[512,1152]{1,0:T(8,128)(2,1)} reshape(bf16[512,12,4,24]{3,2,1,0:T(4,128)(2,1)} %bitcast.129) | data formatting | bytes 2359296
  464.7 27.7 %reduce-scatter.19.cloned.1.call-done = bf16[128,1152]{1,0:T(8,128)(2,1)} async-done(((bf16[512,1152]{1,0:T(8,128)(2,1)}), bf16[128,1152]{1,0:T(8,128)(2,1)}) %reduce-scatter.19.cloned.1.call-update) | async-done | bytes 294928
  492.4 5.3 %reshape.115 = bf16[128,12,4,24]{3,2,1,0:T(4,128)(2,1)S(1)} reshape(bf16[128,1152]{1,0:T(8,128)(2,1)} %reduce-scatter.19.cloned.1.call-done) | data formatting | bytes 589824
  497.7 1.4 copy.235
  499.1 0.8 copy.213
  (107 shorter events, 10.1 us)
Async XLA Ops:
  6.5 97.5 %all-gather.5.cloned.1.call-start = ((), (), s32[]{:S(2)}) async-start(), calls=%async_computation.4 | async-start | bytes 1474560 | tf_op jit(solution)/shard_map/all_gather | solution.py:97
  7.3 164.4 %reduce-scatter.13.cloned.1.call-start = ((), (), s32[]{:S(2)}) async-start(), calls=%async_computation.8 | async-start | bytes 1474560
  48.1 8.3 %copy-start.8 = (s32[144,144]{1,0:T(8,128)S(1)}, s32[144,144]{1,0:T(8,128)}, u32[]{:S(2)}) copy-start(s32[144,144]{1,0:T(8,128)} %param.16) | copy-start | bytes 248836
  104.0 1.9 copy-start.1
  105.9 2.1 copy-start.12
  115.3 1.0 copy-start.9
  139.5 38.8 %copy-start.7 = (bf16[12,24,4,128]{3,2,1,0:T(4,128)(2,1)S(1)}, bf16[12,24,4,128]{3,2,1,0:T(4,128)(2,1)}, u32[]{:S(2)}) copy-start(bf16[12,24,4,128]{3,2,1,0:T(4,128)(2,1)} %param.10) | copy-start | bytes 884740
  139.6 70.2 %all-gather.7.cloned.1.call-start = ((), (), s32[]{:S(2)}) async-start(), calls=%async_computation.5 | async-start | bytes 1474560 | tf_op jit(solution)/shard_map/all_gather | solution.py:123
  179.1 87.6 %reduce-scatter.15.cloned.1.call-start = ((), (), s32[]{:S(2)}) async-start(), calls=%async_computation.9 | async-start | bytes 1474560
  209.7 3.4 copy-start.2
  239.1 34.3 %copy-start.5 = (bf16[12,24,4,128]{3,1,2,0:T(8,128)(2,1)S(1)}, bf16[12,24,4,128]{3,1,2,0:T(8,128)(2,1)}, u32[]{:S(2)}) copy-start(bf16[12,24,4,128]{3,1,2,0:T(8,128)(2,1)} %add_convert_fusion.3) | copy-start | bytes 884740
  239.1 35.4 %copy-start.10 = (s32[12,24,4]{1,2,0:T(4,128)S(1)}, s32[12,24,4]{1,2,0:T(4,128)}, u32[]{:S(2)}) copy-start(s32[12,24,4]{1,2,0:T(4,128)} %param.17) | copy-start | bytes 13828
  239.1 65.8 %all-gather.9.cloned.1.call-start = ((), (), s32[]{:S(2)}) async-start(), calls=%async_computation.6 | async-start | bytes 1474560 | tf_op jit(solution)/shard_map/all_gather | solution.py:97
  274.2 123.1 %reduce-scatter.17.cloned.1.call-start = ((), (), s32[]{:S(2)}) async-start(), calls=%async_computation.10 | async-start | bytes 1474560
  304.9 3.4 copy-start
  308.8 13.0 %collective-permute-start = (bf16[6,24,4,512]{3,1,2,0:T(8,128)(2,1)S(1)}, bf16[6,24,4,512]{3,1,2,0:T(8,128)(2,1)S(1)}, u32[]{:S(2)}, u32[]{:S(2)}) collective-permute-start(bf16[6,24,4,512]{3,1,2,0:T(8,128)(2,1)S(1)} %get-tuple-element.7), channel_id=1, source_target_pairs={{0,24},{8,0},{16,8},{24,16},{1,25},{9,1},{17,9},{25,17},{2,26},{10... | collective-permute-start | bytes 1769480 | tf_op jit(solution)/shard_map/ppermute | solution.py:17
  309.5 7.5 %collective-permute-start.2 = (bf16[6,24,4]{1,2,0:T(4,128)(2,1)S(1)}, bf16[6,24,4]{1,2,0:T(4,128)(2,1)S(1)}, u32[]{:S(2)}, u32[]{:S(2)}) collective-permute-start(bf16[6,24,4]{1,2,0:T(4,128)(2,1)S(1)} %get-tuple-element.19), channel_id=1, source_target_pairs={{0,24},{8,0},{16,8},{24,16},{1,25},{9,1},{17,9},{25,17},{2,26},{10... | collective-permute-start | bytes 3464 | tf_op jit(solution)/shard_map/ppermute | solution.py:17
  317.0 3.8 collective-permute-start.3
  321.9 6.3 %collective-permute-start.1 = (bf16[12,3,4,512]{3,1,2,0:T(4,128)(2,1)S(1)}, bf16[12,3,4,512]{3,1,2,0:T(4,128)(2,1)S(1)}, u32[]{:S(2)}, u32[]{:S(2)}) collective-permute-start(bf16[12,3,4,512]{3,1,2,0:T(4,128)(2,1)S(1)} %pad_maximum_fusion.2), channel_id=1, source_target_pairs={{0,4},{4,0},{1,5},{5,1},{2,6},{6,2},{3,7},{7,3},{8,12},{12,8},{9,1... | collective-permute-start | bytes 442376 | tf_op jit(solution)/shard_map/ppermute | solution.py:17
  323.7 4.7 copy-start.13
  337.1 4.2 collective-permute-start.4
  341.3 4.6 collective-permute-start.5
  369.1 34.9 %copy-start.4 = (bf16[12,24,4,128]{3,1,2,0:T(8,128)(2,1)S(1)}, bf16[12,24,4,128]{3,1,2,0:T(8,128)(2,1)}, u32[]{:S(2)}) copy-start(bf16[12,24,4,128]{3,1,2,0:T(8,128)(2,1)} %add_convert_fusion.2) | copy-start | bytes 884740
  369.2 66.3 %all-gather.11.cloned.1.call-start = ((), (), s32[]{:S(2)}) async-start(), calls=%async_computation.7 | async-start | bytes 1474560 | tf_op jit(solution)/shard_map/all_gather | solution.py:123
  402.6 36.3 %copy-start.11 = (bf16[2,512,512]{2,1,0:T(8,128)(2,1)S(1)}, bf16[2,512,512]{2,1,0:T(8,128)(2,1)}, u32[]{:S(2)}) copy-start(bf16[2,512,512]{2,1,0:T(8,128)(2,1)} %param.14) | copy-start | bytes 3145732
  404.8 87.5 %reduce-scatter.19.cloned.1.call-start = ((), (), s32[]{:S(2)}) async-start(), calls=%async_computation.11 | async-start | bytes 1474560
  435.5 3.4 copy-start.3
  464.7 34.4 %copy-start.6 = (bf16[12,24,4,128]{3,1,2,0:T(8,128)(2,1)S(1)}, bf16[12,24,4,128]{3,1,2,0:T(8,128)(2,1)}, u32[]{:S(2)}) copy-start(bf16[12,24,4,128]{3,1,2,0:T(8,128)(2,1)} %add_convert_fusion.1) | copy-start | bytes 884740
Sparse Core Ops, SparseCore 0:
  8.9 34.4 all-gather.4
  139.7 31.9 reduce-scatter.12
  179.2 30.4 all-gather.6
  239.2 27.4 reduce-scatter.14
  274.4 30.4 all-gather.8
  369.3 28.0 reduce-scatter.16
  405.0 30.4 all-gather.10
  464.8 27.5 reduce-scatter.18
where the time goes:
time: 517 us; the launch traced here: 507 us
  waiting for transfers between devices  228 us (44%)
  local copies, waits for them, and re-layouts  221 us (43%)
  other arithmetic  19.2 us (4%)
  matrix products  17.7 us (3%)
  between operations  14.7 us (3%)
  starting transfers between devices  6.99 us (1%)
    unnamed x47, local copies, waits for them, and re-layouts  118 us
    unnamed x12, waiting for transfers between devices  116 us
    gather x4, local copies, waits for them, and re-layouts, attend(): bias = jnp.take(table, index, axis=0).transpose(2, 0, 1)  94.2 us
    all_gather x2, waiting for transfers between devices, local(): whole = lax.all_gather(state, 'head', axis=3, tiled=True)  61.1 us
    all_gather x2, waiting for transfers between devices, head_features(): whole = lax.all_gather(state, 'head', axis=3, tiled=True)  30.4 us
    ppermute x6, waiting for transfers between devices, passed_along(): lax.ppermute(shard, axis, [(i, (i + by) % size) for i in range(size)])  20.3 us
  transfers between devices with their start and end apart: 14, of which 12 were waited for; matrix products, arithmetic and copies ran while one was open for 19% of the time, Pallas kernels for 0%

commit v1 on v0

v1 whole, which is shorter than its diff:
```python
import functools

import jax
import jax.numpy as jnp
import numpy as np
from jax import lax
from jax.experimental import pallas as pl
from jax.experimental.pallas import tpu as pltpu
from jax.sharding import PartitionSpec as P

WIN_LON = 12
WIN_LAT = 6
WIN_LEV = 2
LEV = 4
TOK = WIN_LON * WIN_LAT * WIN_LEV
ROWS = 2 * TOK
QUAD = 80
EPS = 1e-05
MASKED = -1000000000.0
HEADS_N = 4
MESH = pl.DeviceIdType.MESH


def row_maps():
    to_quads = np.zeros((4 * QUAD, ROWS), np.float32)
    to_rolled = np.zeros((ROWS, 4 * QUAD), np.float32)
    for w in range(2):
        for lon in range(12):
            for lat in range(6):
                for lv in range(2):
                    row = ((w * 12 + lon) * 6 + lat) * 2 + lv
                    lev = 2 * w + lv
                    quad = (lon // 6) * 2 + lat // 3
                    at = quad * QUAD + ((lon % 6) * 3 + lat % 3) * 4 + lev
                    to_quads[at, row] = 1
                    src_lon, src_lat, src_lev = (lon + 6) % 12, (lat + 3) % 6, (lev + 1) % 4
                    quad = (src_lon // 6) * 2 + src_lat // 3
                    at = quad * QUAD + ((src_lon % 6) * 3 + src_lat % 3) * 4 + src_lev
                    to_rolled[row, at] = 1
    return to_quads, to_rolled


def norm(values):
    center = values - jnp.mean(values, axis=-1, keepdims=True)
    spread = jnp.mean(center * center, axis=-1, keepdims=True)
    return (center * lax.rsqrt(spread + EPS)).astype(jnp.bfloat16)


def dot(a, b):
    return jnp.dot(a, b, preferred_element_type=jnp.float32)


def kernel(
    nlon, nlat,
    x_ref, qw_ref, ow_ref, uw_ref, dw_ref, tab_ref, idx_ref, oh_ref, quads_ref, rolled_ref, back_ref,
    out_ref,
    xp, wq, wo, wu, wd, tabs, bias, nb, ho, acc, st, same, hsend, hrecv, ysend,
    own_sem, xs_sem, xr_sem, ts_sem, tr_sem, zs_sem, zr_sem, ps_sem, pr_sem, cs_sem, cr_sem,
    hs_sem, hr_sem, ys_sem, or_sem,
):
    lon, lat, head = lax.axis_index("lon"), lax.axis_index("lat"), lax.axis_index("head")

    def at(d_lon, d_lat, to_head):
        return (lax.rem(lon + d_lon + nlon, nlon), lax.rem(lat + d_lat + nlat, nlat), to_head)

    core = lax.rem(lon, 2)
    xbit = lax.rem(lon // 2, 2)
    ybit = lax.rem(lat, 2)
    x_lon = lon + 2 - 4 * xbit
    y_lat = lat + 1 - 2 * ybit
    c_lon = lon + 1 - 2 * core

    barrier = pltpu.get_barrier_semaphore()
    count = 0
    for d_lon in (-1, 0, 1):
        for d_lat in (-1, 0, 1):
            for k in range(HEADS_N):
                if d_lon == 0 and d_lat == 0 and k == 0:
                    continue
                pl.semaphore_signal(
                    barrier, inc=1, device_id=at(d_lon, d_lat, lax.rem(head + k, HEADS_N)), device_id_type=MESH
                )
                count += 1
    for target in ((x_lon, lat, head), (x_lon, y_lat, head), (lon, y_lat, head)):
        pl.semaphore_signal(barrier, inc=1, device_id=target, device_id_type=MESH)
        count += 1
    pl.semaphore_wait(barrier, count)

    def remote(src, dst, send, recv, target):
        return pltpu.make_async_remote_copy(
            src_ref=src, dst_ref=dst, send_sem=send, recv_sem=recv, device_id=target, device_id_type=MESH
        )

    weights = ((qw_ref, wq), (ow_ref, wo), (uw_ref, wu), (dw_ref, wd))

    def part(ref, which):
        rows = ref.shape[2] // 8
        return pl.ds(pl.multiple_of(which * rows, 16), rows)

    mine = core * 4 + xbit * 2 + ybit
    of_x = core * 4 + (1 - xbit) * 2 + ybit
    of_y = core * 4 + xbit * 2 + 1 - ybit
    of_d = core * 4 + (1 - xbit) * 2 + 1 - ybit

    def x_copy(k):
        to = lax.rem(head + k, HEADS_N)
        return remote(x_ref.at[to], xp.at[head], xs_sem.at[k], xr_sem.at[k], (lon, lat, to))

    def t_copy(k):
        to = lax.rem(head + k, HEADS_N)
        return remote(tab_ref, tabs.at[head], ts_sem.at[k], tr_sem.at[k], (lon, lat, to))

    def z_copy(b, i, k):
        src, dst = weights[i]
        rows = part(dst, mine)
        to = lax.rem(head + k, HEADS_N)
        return remote(
            src.at[b, rows], dst.at[b, head, rows], zs_sem.at[b, i, k - 1], zr_sem.at[b, i, k - 1], (lon, lat, to)
        )

    def source(k):
        return lax.rem(head + HEADS_N - k, HEADS_N)

    def z_landed(b, i, k):
        dst = weights[i][1].at[b, source(k), part(weights[i][1], mine)]
        pltpu.make_async_copy(dst, dst, zr_sem.at[b, i, k - 1]).wait()

    def p_copies(b, i, k):
        ref = weights[i][1].at[b, source(k), part(weights[i][1], mine)]
        targets = ((x_lon, lat, head), (lon, y_lat, head), (x_lon, y_lat, head))
        return [
            remote(ref, ref, ps_sem.at[b, i, k - 1, d], pr_sem.at[b, i, k - 1, d], target)
            for d, target in enumerate(targets)
        ]

    def p_landed(b, i, k):
        for d, which in enumerate((of_x, of_y, of_d)):
            dst = weights[i][1].at[b, source(k), part(weights[i][1], which)]
            pltpu.make_async_copy(dst, dst, pr_sem.at[b, i, k - 1, d]).wait()

    def half(ref, which):
        rows = ref.shape[2] // 2
        return pl.ds(pl.multiple_of(which * rows, 16), rows)

    def c_copy(b, i, k):
        ref = weights[i][1].at[b, source(k), half(weights[i][1], core)]
        return remote(ref, ref, cs_sem.at[b, i, k - 1], cr_sem.at[b, i, k - 1], (c_lon, lat, head))

    def c_landed(b, i, k):
        dst = weights[i][1].at[b, source(k), half(weights[i][1], 1 - core)]
        pltpu.make_async_copy(dst, dst, cr_sem.at[b, i, k - 1]).wait()

    def each_k(body):
        def step(k, carry):
            body(k)
            return carry

        lax.fori_loop(1, HEADS_N, step, 0)

    def own_copies():
        copies = [
            pltpu.make_async_copy(src, dst.at[:, head], own_sem.at[i]) for i, (src, dst) in enumerate(weights)
        ]
        copies.append(pltpu.make_async_copy(x_ref.at[head], xp.at[head], own_sem.at[4]))
        copies.append(pltpu.make_async_copy(tab_ref, tabs.at[head], own_sem.at[5]))
        return copies

    each_k(lambda k: t_copy(k).start())
    each_k(lambda k: x_copy(k).start())
    for b in range(2):
        for i in range(4):
            each_k(lambda k: z_copy(b, i, k).start())
    for copy in own_copies():
        copy.start()
    for copy in own_copies():
        copy.wait()

    def forward_plane(b, i):
        def body(k):
            z_landed(b, i, k)
            for copy in p_copies(b, i, k):
                copy.start()

        each_k(body)

    def forward_core(b, i):
        def body(k):
            p_landed(b, i, k)
            c_copy(b, i, k).start()

        each_k(body)

    def arrived(b, i):
        each_k(lambda k: c_landed(b, i, k))

    def make_bias():
        index = idx_ref[...]
        low = jnp.bitwise_and(index, 127)
        high = jnp.right_shift(index, 7)

        def column(j, carry):
            s, c = j // 4, lax.rem(j, 4)
            for side in range(2):
                lanes = slice(side * 128, side * 128 + 128)
                lo, hi = low[:, lanes], high[:, lanes]
                got = jnp.zeros((TOK, 128), jnp.float32)
                for r in range(6):
                    row = jnp.broadcast_to(tabs[s, c, r : r + 1, :], (TOK, 128))
                    got = jnp.where(hi == r, jnp.take_along_axis(row, lo, axis=1, mode="promise_in_bounds"), got)
                bias[j, :, lanes] = got
            return carry

        lax.fori_loop(0, 16, column, 0)

    def attention(b):
        acc[...] = jnp.zeros_like(acc)

        def shard(s, carry):
            n = nb[...]
            q = dot(n, wq[b, s, 0:512, :]).astype(jnp.bfloat16)
            k = dot(n, wq[b, s, 512:1024, :]).astype(jnp.bfloat16)
            v = dot(n, wq[b, s, 1024:1536, :]).astype(jnp.bfloat16)
            for w in range(2):
                rows = slice(w * TOK, (w + 1) * TOK)
                outs = []
                for hh in range(2):
                    cols = slice(hh * 64, hh * 64 + 64)
                    scores = lax.dot_general(
                        q[rows, cols], k[rows, cols], (((1,), (1,)), ((), ())), preferred_element_type=jnp.float32
                    )
                    scores = scores * 0.125 + bias[s * 4 + b * 2 + hh, :, 0:TOK]
                    if b == 1:
                        scores = jnp.where(same[w] > 0.5, scores, MASKED)
                    expo = jnp.exp(scores - jnp.max(scores, axis=-1, keepdims=True))
                    probs = (expo / jnp.sum(expo, axis=-1, keepdims=True)).astype(jnp.bfloat16)
                    outs.append(dot(probs, v[rows, cols]).astype(jnp.bfloat16))
                ho[rows, :] = jnp.concatenate(outs, axis=1)
            acc[...] += dot(ho[...], wo[b, s])
            return carry

        lax.fori_loop(0, 4, shard, 0)

    def feed_forward(b):
        acc[...] = jnp.zeros_like(acc)

        def shard(s, carry):
            hidden = jax.nn.gelu(dot(nb[...], wu[b, s]), approximate=True).astype(jnp.bfloat16)
            acc[...] += dot(hidden, wd[b, s])
            return carry

        lax.fori_loop(0, 4, shard, 0)

    def add_total():
        st[...] = (st[...].astype(jnp.float32) + acc[...]).astype(jnp.bfloat16)

    def renorm():
        nb[...] = norm(st[...].astype(jnp.float32))

    for b in range(2):
        for i in range(4):
            forward_plane(b, i)
    each_k(lambda k: pltpu.make_async_copy(tabs.at[source(k)], tabs.at[source(k)], tr_sem.at[k]).wait())
    each_k(lambda k: pltpu.make_async_copy(xp.at[source(k)], xp.at[source(k)], xr_sem.at[k]).wait())
    make_bias()
    for b in range(2):
        for i in range(4):
            forward_core(b, i)
    for b in range(2):
        for i in range(4):
            arrived(b, i)

    st[...] = jnp.concatenate([xp[g] for g in range(4)], axis=1)
    renorm()
    attention(0)
    add_total()
    renorm()
    feed_forward(0)
    add_total()

    hsend[:, 0:512] = dot(quads_ref[...], st[...]).astype(jnp.bfloat16)
    hsend[:, 512:640] = oh_ref[...]
    before = lax.rem(head + HEADS_N - 1, HEADS_N)
    lat_back = jnp.where(head == 0, -1, 0)
    lat_next = jnp.where(head == HEADS_N - 1, 1, 0)
    quad_to = (at(-1, lat_back, before), at(-1, 0, head), at(0, lat_back, before))

    def quad_rows(q):
        return pl.ds(q * QUAD, QUAD)

    halo = [
        remote(hsend.at[quad_rows(q)], hrecv.at[quad_rows(q)], hs_sem.at[q], hr_sem.at[q], quad_to[q])
        for q in range(3)
    ]
    for copy in halo:
        copy.start()
    hrecv[3 * QUAD : 4 * QUAD, :] = hsend[3 * QUAD : 4 * QUAD, :]
    for copy in halo:
        copy.wait()

    rolled = dot(rolled_ref[...], hrecv[...]).astype(jnp.bfloat16)
    st[...] = rolled[:, 0:512]
    marks = rolled[:, 512:640]
    for w in range(2):
        of_window = marks[w * TOK : (w + 1) * TOK]
        same[w] = lax.dot_general(
            of_window, of_window, (((1,), (1,)), ((), ())), preferred_element_type=jnp.float32
        )
    renorm()
    attention(1)
    add_total()
    renorm()
    feed_forward(1)
    add_total()

    final = dot(back_ref[...], st[...]).astype(jnp.bfloat16)
    for f in range(4):
        ysend[f] = final[:, f * 128 : (f + 1) * 128]
    after = lax.rem(head + 1, HEADS_N)
    homes = ((1, lat_next, after), (1, 0, head), (0, lat_next, after), (0, 0, head))

    def y_copy(q, k):
        d_lon, d_lat, slot = homes[q]
        to = lax.rem(head + k, HEADS_N)
        return remote(
            ysend.at[to, quad_rows(q)], out_ref.at[slot, quad_rows(q)], ys_sem.at[q, k], or_sem.at[slot, q],
            at(d_lon, d_lat, to),
        )

    def y_local(q):
        slot = homes[q][2]
        return pltpu.make_async_copy(
            ysend.at[head, quad_rows(q)], out_ref.at[slot, quad_rows(q)], or_sem.at[slot, q]
        )

    for q in range(4):
        each_k(lambda k: y_copy(q, k).start())
    for q in (0, 1):
        y_copy(q, 0).start()
    y_local(3).start()

    @pl.when(head < HEADS_N - 1)
    def _():
        y_local(2).start()

    @pl.when(head == HEADS_N - 1)
    def _():
        y_copy(2, 0).start()

    each_k(lambda k: t_copy(k).wait_send())
    each_k(lambda k: x_copy(k).wait_send())
    for b in range(2):
        for i in range(4):

            def sent(k):
                z_copy(b, i, k).wait_send()
                for copy in p_copies(b, i, k):
                    copy.wait_send()
                c_copy(b, i, k).wait_send()

            each_k(sent)
    for q in range(4):
        each_k(lambda k: y_copy(q, k).wait_send())
    for q in (0, 1):
        y_copy(q, 0).wait_send()

    @pl.when(head == HEADS_N - 1)
    def _():
        y_copy(2, 0).wait_send()

    for g in range(4):
        for q in range(4):
            dst = out_ref.at[g, quad_rows(q)]
            pltpu.make_async_copy(dst, dst, or_sem.at[g, q]).wait()


def local(
    nlon, nlat, tokens, qkv_weight, out_weight, up_weight, down_weight, bias_table, bias_index, regions
):
    bf16 = jnp.bfloat16
    head = lax.axis_index("head")
    to_quads, to_rolled = row_maps()
    x = tokens.reshape(12, 4, 6, 2, 2, 128).transpose(1, 3, 0, 2, 4, 5).reshape(4, ROWS, 128)
    table = jnp.pad(bias_table, ((0, 0), (0, 1024 - bias_table.shape[1]), (0, 0)))
    table = table.transpose(0, 2, 1).reshape(4, 8, 128)
    index = jnp.pad(bias_index, ((0, 0), (0, 256 - TOK)))
    ids = lax.dynamic_slice_in_dim(regions, head * 6, 6, axis=1)
    ids = ids.reshape(2, 6, 2, 3, 4).transpose(0, 2, 1, 3, 4).reshape(4, 72)
    ids = jnp.pad(ids, ((0, 0), (0, QUAD - 72))).reshape(4 * QUAD, 1)
    marks = (ids == jnp.arange(128, dtype=jnp.int32)[None, :]).astype(bf16)
    sems = pltpu.SemaphoreType.DMA
    vm = pltpu.VMEM
    any_space = pl.BlockSpec(memory_space=pl.ANY)
    in_vmem = pl.BlockSpec(memory_space=pltpu.VMEM)
    out = pl.pallas_call(
        functools.partial(kernel, nlon, nlat),
        out_shape=jax.ShapeDtypeStruct((4, 4 * QUAD, 128), bf16),
        in_specs=[any_space] * 6 + [in_vmem] * 5,
        out_specs=any_space,
        scratch_shapes=[
            vm((4, ROWS, 128), bf16),
            vm((2, 4, 1536, 128), bf16),
            vm((2, 4, 128, 512), bf16),
            vm((2, 4, 512, 512), bf16),
            vm((2, 4, 512, 512), bf16),
            vm((4, 4, 8, 128), jnp.float32),
            vm((16, TOK, 256), jnp.float32),
            vm((ROWS, 512), bf16),
            vm((ROWS, 128), bf16),
            vm((ROWS, 512), jnp.float32),
            vm((ROWS, 512), bf16),
            vm((2, TOK, TOK), jnp.float32),
            vm((4 * QUAD, 640), bf16),
            vm((4 * QUAD, 640), bf16),
            vm((4, 4 * QUAD, 128), bf16),
            sems((6,)),
            sems((4,)),
            sems((4,)),
            sems((4,)),
            sems((4,)),
            sems((2, 4, 3)),
            sems((2, 4, 3)),
            sems((2, 4, 3, 3)),
            sems((2, 4, 3, 3)),
            sems((2, 4, 3)),
            sems((2, 4, 3)),
            sems((3,)),
            sems((3,)),
            sems((4, 4)),
            sems((4, 4)),
        ],
        compiler_params=pltpu.CompilerParams(
            collective_id=0, has_side_effects=True, vmem_limit_bytes=48 * 1024 * 1024
        ),
        name="swin_pair",
    )(
        x,
        qkv_weight.reshape(2, 1536, 128),
        out_weight,
        up_weight,
        down_weight,
        table,
        index,
        marks,
        jnp.asarray(to_quads, bf16),
        jnp.asarray(to_rolled, bf16),
        jnp.asarray(to_rolled.T, bf16),
    )
    out = out.reshape(4, 4, QUAD, 128)[:, :, :72].reshape(4, 2, 2, 6, 3, 4, 128)
    return out.transpose(1, 3, 0, 2, 4, 5, 6).reshape(12, 24, 4, 128)


def solution(mesh):
    return jax.shard_map(
        functools.partial(local, mesh.shape["lon"], mesh.shape["lat"]),
        mesh=mesh,
        in_specs=(
            P("lon", "lat", None, "head"),
            P(None, None, None, "head"),
            P(None, "head", None),
            P(None, None, "head"),
            P(None, "head", None),
            P(None, None, "head"),
            P(),
            P("lon", "lat", None),
        ),
        out_specs=P("lon", "lat", None, "head"),
        check_vma=False,
    )
```

time: 517 us -> 124 us (0.24); the launches traced: 507 us -> 123 us
  waiting for transfers between devices: 228 us -> 0 us
  local copies, waits for them, and re-layouts: 221 us -> 9.58 us
  Pallas kernels: 0 us -> 114 us
  other arithmetic: 19.2 us -> 0.12 us
  matrix products: 17.7 us -> 0 us
  between operations: 14.7 us -> 0.09 us
  starting transfers between devices: 6.99 us -> 0 us
    unnamed x12 -> x0, waiting for transfers between devices: 116 us -> none
    pallas_call x0 -> x1, Pallas kernels: none -> 114 us  [local(): pl.pallas_call(functools.partial(kernel, nlon, nlat), out_shape=jax.Shape...]
    unnamed x47 -> x18, local copies, waits for them, and re-layouts: 118 us -> 5.91 us
    gather x4 -> x0, local copies, waits for them, and re-layouts: 94.2 us -> none  [attend(): bias = jnp.take(table, index, axis=0).transpose(2, 0, 1)]
    all_gather x4 -> x0, waiting for transfers between devices: 91.5 us -> none  [the longest x2 61.1 us: local(): whole = lax.all_gather(state, 'head', axis=3, tiled=True)]
    ppermute x6 -> x0, waiting for transfers between devices: 20.3 us -> none  [passed_along(): lax.ppermute(shard, axis, [(i, (i + by) % size) for i in range(size)])]
    reduce_sum x8 -> x0, other arithmetic: 13.2 us -> none  [the longest x4 6.7 us: layer_norm(): center = values - jnp.mean(values, axis=-1, keepdims=True)]
    dot_general x8 -> x0, matrix products: 12.9 us -> none  [the longest x2 6.21 us: local(): jnp.einsum('lavf,fd->lavd', hidden, down_weight[block], preferred_element...]
  transfers between devices with their start and end apart: 14 -> 0, of which waited for: 12 -> 0; matrix products, arithmetic and copies ran while one was open for 19% -> 0% of each run, Pallas kernels for 0% -> 0%
where the time goes in v1:
time: 124 us; the launch traced here: 123 us
  Pallas kernels  114 us (92%)
  local copies, waits for them, and re-layouts  9.58 us (8%)
    pallas_call x1, Pallas kernels, local(): pl.pallas_call(functools.partial(kernel, nlon, nlat), out_shape=jax.Shape...  114 us
    unnamed x18, local copies, waits for them, and re-layouts  5.91 us

profile of v1, /device:TPU:0, one launch (start us, length us, event | category | flops | bytes accessed | tf_op | source)
XLA Modules:
  0.0 123.4 jit_solution(10261257290365738145)
XLA Ops:
  0.0 0.0 copy-start
  0.0 0.0 copy-start.8
  0.0 0.0 copy-start.1
  0.0 0.7 copy-done.8
  0.7 0.0 copy-done
  0.8 0.1 constant_dynamic-slice_fusion
  0.8 0.1 copy.15
  0.9 0.1 reshape.33
  1.0 0.2 copy.16
  1.2 0.1 reshape.34
  1.4 0.1 eq.15
  1.4 0.1 fusion.oh_ref
  1.6 0.9 pad.13.idx_ref
  2.5 0.0 copy-start.5
  2.5 1.2 copy.14
  3.7 0.0 copy-done.1
  3.7 0.0 copy-done.5
  3.7 0.0 copy-start.2
  3.7 1.2 copy-done.2
  5.0 0.0 copy-start.3
  5.0 1.1 copy-done.3
  6.1 0.0 copy-start.4
  6.1 0.9 copy-done.4
  7.0 0.0 copy-start.6
  7.0 0.9 copy-done.6
  8.0 0.0 copy-start.7
  8.0 0.9 copy-done.7
  8.9 113.6 %swin_pair.1 = bf16[4,320,128]{2,1,0:T(8,128)(2,1)S(1)} custom-call(bf16[4,288,128]{2,1,0:T(8,128)(2,1)S(1)} %bitcast.16, bf16[2,1536,128]{2,1,0:T(8,128)(2,1)S(1)} %bitcast.17, bf16[2,128,512]{2,1,0:T(8,128)(2,1)S(1)} %copy-done.4, bf16[2,512,512]{2,1,0:T(8,128)(2,1)S(1)} %copy-done.1, bf16[2,512,512]{2,1,0:T(8,128)(2,1)S(1)} %copy-done.2, ...), custom_call_target="tpu_custom_call" | custom-call | tf_op jit(solution)/shard_map/swin_pair/pallas_call | solution.py:394
  122.6 0.8 copy.17
  (4 shorter events, 0.1 us)
Async XLA Ops:
  0.0 0.8 copy-start
  0.0 0.7 copy-start.8
  0.0 3.7 %copy-start.1 = (bf16[2,512,512]{2,1,0:T(8,128)(2,1)S(1)}, bf16[2,512,512]{2,1,0:T(8,128)(2,1)}, u32[]{:S(2)}) copy-start(bf16[2,512,512]{2,1,0:T(8,128)(2,1)} %uw_ref.1) | copy-start | bytes 3145732
  2.5 1.2 %copy-start.5 = (bf16[320,288]{1,0:T(8,128)(2,1)S(1)}, bf16[320,288]{1,0:T(8,128)(2,1)}, u32[]{:S(2)}) copy-start(bf16[320,288]{1,0:T(8,128)(2,1)} %constant.20.clone.back_ref) | copy-start | bytes 552964
  3.7 1.2 copy-start.2
  5.0 1.1 copy-start.3
  6.1 0.9 copy-start.4
  7.0 0.9 copy-start.6
  8.0 0.9 copy-start.7

commit v2 on v1

--- a/solution.py
+++ b/solution.py
@@ -52,9 +52,9 @@
 
 def kernel(
     nlon, nlat,
-    x_ref, qw_ref, ow_ref, uw_ref, dw_ref, tab_ref, idx_ref, oh_ref, quads_ref, rolled_ref, back_ref,
+    x_ref, qw_ref, ow_ref, uw_ref, dw_ref, tab_ref, idx_hbm, oh_hbm, quads_hbm, rolled_hbm, back_hbm,
     out_ref,
-    xp, wq, wo, wu, wd, tabs, bias, nb, ho, acc, st, same, hsend, hrecv, ysend,
+    idx_ref, quads_ref, rolled_ref, back_ref, xp, wq, wo, wu, wd, tabs, bias, nb, ho, acc, st, same, hsend, hrecv, ysend,
     own_sem, xs_sem, xr_sem, ts_sem, tr_sem, zs_sem, zr_sem, ps_sem, pr_sem, cs_sem, cr_sem,
     hs_sem, hr_sem, ys_sem, or_sem,
 ):
@@ -84,7 +84,6 @@
     for target in ((x_lon, lat, head), (x_lon, y_lat, head), (lon, y_lat, head)):
         pl.semaphore_signal(barrier, inc=1, device_id=target, device_id_type=MESH)
         count += 1
-    pl.semaphore_wait(barrier, count)
 
     def remote(src, dst, send, recv, target):
         return pltpu.make_async_remote_copy(
@@ -127,16 +126,20 @@
 
     def p_copies(b, i, k):
         ref = weights[i][1].at[b, source(k), part(weights[i][1], mine)]
-        targets = ((x_lon, lat, head), (lon, y_lat, head), (x_lon, y_lat, head))
         return [
             remote(ref, ref, ps_sem.at[b, i, k - 1, d], pr_sem.at[b, i, k - 1, d], target)
-            for d, target in enumerate(targets)
+            for d, target in enumerate(((x_lon, lat, head), (lon, y_lat, head)))
         ]
 
-    def p_landed(b, i, k):
-        for d, which in enumerate((of_x, of_y, of_d)):
-            dst = weights[i][1].at[b, source(k), part(weights[i][1], which)]
-            pltpu.make_async_copy(dst, dst, pr_sem.at[b, i, k - 1, d]).wait()
+    def p_landed(b, i, k, d):
+        dst = weights[i][1].at[b, source(k), part(weights[i][1], (of_x, of_y, of_d)[d])]
+        pltpu.make_async_copy(dst, dst, pr_sem.at[b, i, k - 1, d]).wait()
+
+    def d_copy(b, i, k):
+        by_x = lax.rem(b + i + k, 2)
+        ref = weights[i][1].at[b, source(k), part(weights[i][1], by_x * of_x + (1 - by_x) * of_y)]
+        target = (by_x * lon + (1 - by_x) * x_lon, by_x * y_lat + (1 - by_x) * lat, head)
+        return remote(ref, ref, ps_sem.at[b, i, k - 1, 2], pr_sem.at[b, i, k - 1, 2], target)
 
     def half(ref, which):
         rows = ref.shape[2] // 2
@@ -163,16 +166,23 @@
         ]
         copies.append(pltpu.make_async_copy(x_ref.at[head], xp.at[head], own_sem.at[4]))
         copies.append(pltpu.make_async_copy(tab_ref, tabs.at[head], own_sem.at[5]))
+        small = (
+            (idx_hbm, idx_ref), (quads_hbm, quads_ref), (rolled_hbm, rolled_ref), (back_hbm, back_ref),
+            (oh_hbm, hsend.at[:, 512:640]),
+        )
+        for i, (src, dst) in enumerate(small):
+            copies.append(pltpu.make_async_copy(src, dst, own_sem.at[6 + i]))
         return copies
 
+    for copy in own_copies():
+        copy.start()
+    pl.semaphore_wait(barrier, count)
     each_k(lambda k: t_copy(k).start())
     each_k(lambda k: x_copy(k).start())
     for b in range(2):
         for i in range(4):
             each_k(lambda k: z_copy(b, i, k).start())
     for copy in own_copies():
-        copy.start()
-    for copy in own_copies():
         copy.wait()
 
     def forward_plane(b, i):
@@ -183,72 +193,83 @@
 
         each_k(body)
 
+    def forward_diagonal(b, i):
+        def body(k):
+            p_landed(b, i, k, 0)
+            p_landed(b, i, k, 1)
+            d_copy(b, i, k).start()
+
+        each_k(body)
+
     def forward_core(b, i):
         def body(k):
-            p_landed(b, i, k)
+            p_landed(b, i, k, 2)
             c_copy(b, i, k).start()
 
         each_k(body)
 
-    def arrived(b, i):
-        each_k(lambda k: c_landed(b, i, k))
-
-    def make_bias():
+    def plan():
+        order = [(b, i) for b in range(2) for i in range(4)]
+        for step in range(len(order) + 2):
+            for late, forward in enumerate((forward_plane, forward_diagonal, forward_core)):
+                if 0 <= step - late < len(order):
+                    yield forward, order[step - late]
+
+    pending = list(plan())
+
+    def pump(count):
+        for forward, (b, i) in pending[:count]:
+            forward(b, i)
+        del pending[:count]
+
+    def make_bias(k):
+        s = source(k)
         index = idx_ref[...]
-        low = jnp.bitwise_and(index, 127)
-        high = jnp.right_shift(index, 7)
-
-        def column(j, carry):
-            s, c = j // 4, lax.rem(j, 4)
-            for side in range(2):
-                lanes = slice(side * 128, side * 128 + 128)
-                lo, hi = low[:, lanes], high[:, lanes]
+        edge = jnp.concatenate([index[:, 128:], jnp.zeros((TOK, 256 - TOK), jnp.int32)], axis=1)
+
+        def column(c, carry):
+            for side, part_index in enumerate((index[:, :128], edge)):
+                lo = jnp.bitwise_and(part_index, 127)
+                hi = jnp.right_shift(part_index, 7)
                 got = jnp.zeros((TOK, 128), jnp.float32)
                 for r in range(6):
                     row = jnp.broadcast_to(tabs[s, c, r : r + 1, :], (TOK, 128))
                     got = jnp.where(hi == r, jnp.take_along_axis(row, lo, axis=1, mode="promise_in_bounds"), got)
-                bias[j, :, lanes] = got
+                bias[s * 4 + c, :, side * 128 : side * 128 + 128] = got
             return carry
 
-        lax.fori_loop(0, 16, column, 0)
-
-    def attention(b):
-        acc[...] = jnp.zeros_like(acc)
-
-        def shard(s, carry):
-            n = nb[...]
-            q = dot(n, wq[b, s, 0:512, :]).astype(jnp.bfloat16)
-            k = dot(n, wq[b, s, 512:1024, :]).astype(jnp.bfloat16)
-            v = dot(n, wq[b, s, 1024:1536, :]).astype(jnp.bfloat16)
-            for w in range(2):
-                rows = slice(w * TOK, (w + 1) * TOK)
-                outs = []
-                for hh in range(2):
-                    cols = slice(hh * 64, hh * 64 + 64)
-                    scores = lax.dot_general(
-                        q[rows, cols], k[rows, cols], (((1,), (1,)), ((), ())), preferred_element_type=jnp.float32
-                    )
-                    scores = scores * 0.125 + bias[s * 4 + b * 2 + hh, :, 0:TOK]
-                    if b == 1:
-                        scores = jnp.where(same[w] > 0.5, scores, MASKED)
-                    expo = jnp.exp(scores - jnp.max(scores, axis=-1, keepdims=True))
-                    probs = (expo / jnp.sum(expo, axis=-1, keepdims=True)).astype(jnp.bfloat16)
-                    outs.append(dot(probs, v[rows, cols]).astype(jnp.bfloat16))
-                ho[rows, :] = jnp.concatenate(outs, axis=1)
-            acc[...] += dot(ho[...], wo[b, s])
-            return carry
-
-        lax.fori_loop(0, 4, shard, 0)
-
-    def feed_forward(b):
-        acc[...] = jnp.zeros_like(acc)
-
-        def shard(s, carry):
-            hidden = jax.nn.gelu(dot(nb[...], wu[b, s]), approximate=True).astype(jnp.bfloat16)
-            acc[...] += dot(hidden, wd[b, s])
-            return carry
-
-        lax.fori_loop(0, 4, shard, 0)
+        lax.fori_loop(0, 4, column, 0)
+
+    def attention(b, k):
+        s = source(k)
+        n = nb[...]
+        query = dot(n, wq[b, s, 0:512, :]).astype(jnp.bfloat16)
+        keys = dot(n, wq[b, s, 512:1024, :]).astype(jnp.bfloat16)
+        v = dot(n, wq[b, s, 1024:1536, :]).astype(jnp.bfloat16)
+        for w in range(2):
+            rows = slice(w * TOK, (w + 1) * TOK)
+            outs = []
+            for hh in range(2):
+                cols = slice(hh * 64, hh * 64 + 64)
+                scores = lax.dot_general(
+                    query[rows, cols], keys[rows, cols], (((1,), (1,)), ((), ())),
+                    preferred_element_type=jnp.float32,
+                )
+                scores = scores * 0.125 + bias[s * 4 + b * 2 + hh, :, 0:TOK]
+                if b == 1:
+                    scores = jnp.where(same[w] > 0.5, scores, MASKED)
+                expo = jnp.exp(scores - jnp.max(scores, axis=-1, keepdims=True))
+                probs = (expo / jnp.sum(expo, axis=-1, keepdims=True)).astype(jnp.bfloat16)
+                outs.append(dot(probs, v[rows, cols]).astype(jnp.bfloat16))
+            ho[rows, :] = jnp.concatenate(outs, axis=1)
+        total = dot(ho[...], wo[b, s])
+        acc[...] = total if k == 0 else acc[...] + total
+
+    def feed_forward(b, k):
+        s = source(k)
+        hidden = jax.nn.gelu(dot(nb[...], wu[b, s]), approximate=True).astype(jnp.bfloat16)
+        total = dot(hidden, wd[b, s])
+        acc[...] = total if k == 0 else acc[...] + total
 
     def add_total():
         st[...] = (st[...].astype(jnp.float32) + acc[...]).astype(jnp.bfloat16)
@@ -256,29 +277,36 @@
     def renorm():
         nb[...] = norm(st[...].astype(jnp.float32))
 
-    for b in range(2):
-        for i in range(4):
-            forward_plane(b, i)
-    each_k(lambda k: pltpu.make_async_copy(tabs.at[source(k)], tabs.at[source(k)], tr_sem.at[k]).wait())
+    pump(1)
     each_k(lambda k: pltpu.make_async_copy(xp.at[source(k)], xp.at[source(k)], xr_sem.at[k]).wait())
-    make_bias()
-    for b in range(2):
-        for i in range(4):
-            forward_core(b, i)
-    for b in range(2):
-        for i in range(4):
-            arrived(b, i)
-
     st[...] = jnp.concatenate([xp[g] for g in range(4)], axis=1)
     renorm()
-    attention(0)
+    pump(2)
+    make_bias(0)
+    pump(3)
+    attention(0, 0)
+    pump(3)
+    each_k(lambda k: pltpu.make_async_copy(tabs.at[source(k)], tabs.at[source(k)], tr_sem.at[k]).wait())
+    make_bias(1)
+    pump(3)
+    make_bias(2)
+    make_bias(3)
+    for k in range(1, 4):
+        c_landed(0, 0, k)
+        c_landed(0, 1, k)
+        attention(0, k)
+        pump(2)
     add_total()
     renorm()
-    feed_forward(0)
+    for k in range(4):
+        if k > 0:
+            c_landed(0, 2, k)
+            c_landed(0, 3, k)
+        feed_forward(0, k)
+        pump(2)
     add_total()
 
     hsend[:, 0:512] = dot(quads_ref[...], st[...]).astype(jnp.bfloat16)
-    hsend[:, 512:640] = oh_ref[...]
     before = lax.rem(head + HEADS_N - 1, HEADS_N)
     lat_back = jnp.where(head == 0, -1, 0)
     lat_next = jnp.where(head == HEADS_N - 1, 1, 0)
@@ -306,10 +334,19 @@
             of_window, of_window, (((1,), (1,)), ((), ())), preferred_element_type=jnp.float32
         )
     renorm()
-    attention(1)
+    attention(1, 0)
+    pump(len(pending))
+    for k in range(1, 4):
+        c_landed(1, 0, k)
+        c_landed(1, 1, k)
+        attention(1, k)
     add_total()
     renorm()
-    feed_forward(1)
+    for k in range(4):
+        if k > 0:
+            c_landed(1, 2, k)
+            c_landed(1, 3, k)
+        feed_forward(1, k)
     add_total()
 
     final = dot(back_ref[...], st[...]).astype(jnp.bfloat16)
@@ -355,6 +392,7 @@
                 z_copy(b, i, k).wait_send()
                 for copy in p_copies(b, i, k):
                     copy.wait_send()
+                d_copy(b, i, k).wait_send()
                 c_copy(b, i, k).wait_send()
 
             each_k(sent)
@@ -382,7 +420,6 @@
     x = tokens.reshape(12, 4, 6, 2, 2, 128).transpose(1, 3, 0, 2, 4, 5).reshape(4, ROWS, 128)
     table = jnp.pad(bias_table, ((0, 0), (0, 1024 - bias_table.shape[1]), (0, 0)))
     table = table.transpose(0, 2, 1).reshape(4, 8, 128)
-    index = jnp.pad(bias_index, ((0, 0), (0, 256 - TOK)))
     ids = lax.dynamic_slice_in_dim(regions, head * 6, 6, axis=1)
     ids = ids.reshape(2, 6, 2, 3, 4).transpose(0, 2, 1, 3, 4).reshape(4, 72)
     ids = jnp.pad(ids, ((0, 0), (0, QUAD - 72))).reshape(4 * QUAD, 1)
@@ -390,13 +427,17 @@
     sems = pltpu.SemaphoreType.DMA
     vm = pltpu.VMEM
     any_space = pl.BlockSpec(memory_space=pl.ANY)
-    in_vmem = pl.BlockSpec(memory_space=pltpu.VMEM)
+    in_hbm = pl.BlockSpec(memory_space=pltpu.HBM)
     out = pl.pallas_call(
         functools.partial(kernel, nlon, nlat),
         out_shape=jax.ShapeDtypeStruct((4, 4 * QUAD, 128), bf16),
-        in_specs=[any_space] * 6 + [in_vmem] * 5,
+        in_specs=[any_space] + [in_hbm] * 4 + [any_space] + [in_hbm] + [any_space] + [in_hbm] * 3,
         out_specs=any_space,
         scratch_shapes=[
+            vm((TOK, TOK), jnp.int32),
+            vm((4 * QUAD, ROWS), bf16),
+            vm((ROWS, 4 * QUAD), bf16),
+            vm((4 * QUAD, ROWS), bf16),
             vm((4, ROWS, 128), bf16),
             vm((2, 4, 1536, 128), bf16),
             vm((2, 4, 128, 512), bf16),
@@ -412,7 +453,7 @@
             vm((4 * QUAD, 640), bf16),
             vm((4 * QUAD, 640), bf16),
             vm((4, 4 * QUAD, 128), bf16),
-            sems((6,)),
+            sems((11,)),
             sems((4,)),
             sems((4,)),
             sems((4,)),
@@ -439,7 +480,7 @@
         up_weight,
         down_weight,
         table,
-        index,
+        bias_index,
         marks,
         jnp.asarray(to_quads, bf16),
         jnp.asarray(to_rolled, bf16),

time: 124 us -> 110 us (0.89)
  Pallas kernels: 114 us -> 99.9 us
    pallas_call x1, Pallas kernels: 114 us -> 99.9 us  [local(): pl.pallas_call(functools.partial(kernel, nlon, nlat), out_shape=jax.Shape...]
where the time goes in v2:
time: 110 us
  Pallas kernels  99.9 us (91%)
  local copies, waits for them, and re-layouts  9.72 us (9%)
    pallas_call x1, Pallas kernels, local(): pl.pallas_call(functools.partial(kernel, nlon, nlat), out_shape=jax.Shape...  99.9 us
    unnamed x18, local copies, waits for them, and re-layouts  6.21 us

profile of v2, /device:TPU:0, one launch (start us, length us, event | category | flops | bytes accessed | tf_op | source)
XLA Modules:
  0.0 109.8 jit_solution(4032391689365922106)
XLA Ops:
  0.0 0.0 copy-start
  0.0 0.0 copy-start.3
  0.0 0.8 pad_bitcast_fusion
  0.8 0.0 copy-done
  0.8 0.1 constant_dynamic-slice_fusion
  0.9 0.1 copy.15
  1.0 0.1 reshape.33
  1.1 0.2 copy.16
  1.3 0.1 reshape.34
  1.4 0.1 eq.15
  1.5 0.1 fusion.oh_hbm
  1.6 0.0 copy-start.7
  1.6 1.2 %copy.14 = bf16[12,4,6,2,2,128]{5,4,2,0,3,1:T(2,128)(2,1)S(1)} copy(bf16[12,4,6,2,2,128]{5,4,3,2,1,0:T(2,128)(2,1)} %bitcast.19) | data formatting | bytes 589824 | tf_op jit(solution)/shard_map/reshape | solution.py:420
  2.8 0.0 copy-done.3
  2.9 0.0 copy-done.7
  2.9 0.0 copy-start.1
  2.9 1.2 %copy-done.1 = bf16[2,512,512]{2,1,0:T(8,128)(2,1)S(1)} copy-done((bf16[2,512,512]{2,1,0:T(8,128)(2,1)S(1)}, bf16[2,512,512]{2,1,0:T(8,128)(2,1)}, u32[]{:S(2)}) %copy-start.1) | copy-done | bytes 1048600
  4.1 0.0 copy-start.2
  4.1 1.2 %copy-done.2 = bf16[2,512,512]{2,1,0:T(8,128)(2,1)S(1)} copy-done((bf16[2,512,512]{2,1,0:T(8,128)(2,1)S(1)}, bf16[2,512,512]{2,1,0:T(8,128)(2,1)}, u32[]{:S(2)}) %copy-start.2) | copy-done | bytes 1048600
  5.3 0.0 copy-start.4
  5.3 0.9 copy-done.4
  6.3 0.0 copy-start.5
  6.3 0.9 copy-done.5
  7.2 0.0 copy-start.6
  7.2 0.9 copy-done.6
  8.2 0.0 copy-start.8
  8.2 0.9 copy-done.8
  9.1 99.9 %swin_pair.1 = bf16[4,320,128]{2,1,0:T(8,128)(2,1)S(1)} custom-call(bf16[4,288,128]{2,1,0:T(8,128)(2,1)S(1)} %bitcast.16, bf16[2,1536,128]{2,1,0:T(8,128)(2,1)S(1)} %bitcast.17, bf16[2,128,512]{2,1,0:T(8,128)(2,1)S(1)} %copy-done.4, bf16[2,512,512]{2,1,0:T(8,128)(2,1)S(1)} %copy-done.1, bf16[2,512,512]{2,1,0:T(8,128)(2,1)S(1)} %copy-done.2, ...), custom_call_target="tpu_custom_call" | custom-call | tf_op jit(solution)/shard_map/swin_pair/pallas_call | solution.py:431
  109.0 0.8 copy.17
  (3 shorter events, 0.0 us)
Async XLA Ops:
  0.0 0.8 copy-start
  0.0 2.8 %copy-start.3 = (bf16[2,3,512,128]{3,2,1,0:T(8,128)(2,1)S(1)}, bf16[2,3,512,128]{3,2,1,0:T(8,128)(2,1)}, u32[]{:S(2)}) copy-start(bf16[2,3,512,128]{3,2,1,0:T(8,128)(2,1)} %param.12) | copy-start | bytes 2359300
  1.6 1.2 %copy-start.7 = (bf16[288,320]{1,0:T(8,128)(2,1)S(1)}, bf16[288,320]{1,0:T(8,128)(2,1)}, u32[]{:S(2)}) copy-start(bf16[288,320]{1,0:T(8,128)(2,1)} %constant.19.clone.rolled_hbm) | copy-start | bytes 552964
  2.9 1.2 %copy-start.1 = (bf16[2,512,512]{2,1,0:T(8,128)(2,1)S(1)}, bf16[2,512,512]{2,1,0:T(8,128)(2,1)}, u32[]{:S(2)}) copy-start(bf16[2,512,512]{2,1,0:T(8,128)(2,1)} %uw_ref.1) | copy-start | bytes 3145732
  4.1 1.2 %copy-start.2 = (bf16[2,512,512]{2,1,0:T(8,128)(2,1)S(1)}, bf16[2,512,512]{2,1,0:T(8,128)(2,1)}, u32[]{:S(2)}) copy-start(bf16[2,512,512]{2,1,0:T(8,128)(2,1)} %dw_ref.1) | copy-start | bytes 3145732
  5.3 0.9 copy-start.4
  6.3 0.9 copy-start.5
  7.2 0.9 copy-start.6
  8.2 0.9 copy-start.8

commit v3 on v2

--- a/solution.py
+++ b/solution.py
@@ -179,9 +179,15 @@
     pl.semaphore_wait(barrier, count)
     each_k(lambda k: t_copy(k).start())
     each_k(lambda k: x_copy(k).start())
-    for b in range(2):
-        for i in range(4):
-            each_k(lambda k: z_copy(b, i, k).start())
+    order = [(b, i) for b in range(2) for i in range(4)]
+    ahead = 2
+
+    def send_along_z(t):
+        if t < len(order):
+            each_k(lambda k: z_copy(*order[t], k).start())
+
+    for t in range(ahead):
+        send_along_z(t)
     for copy in own_copies():
         copy.wait()
 
@@ -192,6 +198,7 @@
                 copy.start()
 
         each_k(body)
+        send_along_z(order.index((b, i)) + ahead)
 
     def forward_diagonal(b, i):
         def body(k):
@@ -209,7 +216,6 @@
         each_k(body)
 
     def plan():
-        order = [(b, i) for b in range(2) for i in range(4)]
         for step in range(len(order) + 2):
             for late, forward in enumerate((forward_plane, forward_diagonal, forward_core)):
                 if 0 <= step - late < len(order):
@@ -295,7 +301,7 @@
         c_landed(0, 0, k)
         c_landed(0, 1, k)
         attention(0, k)
-        pump(2)
+        pump(1)
     add_total()
     renorm()
     for k in range(4):
@@ -303,7 +309,7 @@
             c_landed(0, 2, k)
             c_landed(0, 3, k)
         feed_forward(0, k)
-        pump(2)
+        pump(1)
     add_total()
 
     hsend[:, 0:512] = dot(quads_ref[...], st[...]).astype(jnp.bfloat16)
@@ -322,6 +328,7 @@
     for copy in halo:
         copy.start()
     hrecv[3 * QUAD : 4 * QUAD, :] = hsend[3 * QUAD : 4 * QUAD, :]
+    pump(2)
     for copy in halo:
         copy.wait()
 
@@ -335,11 +342,12 @@
         )
     renorm()
     attention(1, 0)
-    pump(len(pending))
+    pump(1)
     for k in range(1, 4):
         c_landed(1, 0, k)
         c_landed(1, 1, k)
         attention(1, k)
+        pump(1)
     add_total()
     renorm()
     for k in range(4):

time: 110 us -> 98.9 us (0.90)
  Pallas kernels: 99.9 us -> 88.7 us
    pallas_call x1, Pallas kernels: 99.9 us -> 88.7 us  [local(): pl.pallas_call(functools.partial(kernel, nlon, nlat), out_shape=jax.Shape...]
where the time goes in v3:
time: 98.9 us; the launch traced here: 98.6 us
  Pallas kernels  88.7 us (90%)
  local copies, waits for them, and re-layouts  9.72 us (10%)
    pallas_call x1, Pallas kernels, local(): pl.pallas_call(functools.partial(kernel, nlon, nlat), out_shape=jax.Shape...  88.7 us
    unnamed x18, local copies, waits for them, and re-layouts  6.21 us

profile of v3, /device:TPU:0, one launch (start us, length us, event | category | flops | bytes accessed | tf_op | source)
XLA Modules:
  0.0 98.6 jit_solution(10585376174410910965)
XLA Ops:
  0.0 0.0 copy-start
  0.0 0.0 copy-start.3
  0.0 0.8 pad_bitcast_fusion
  0.8 0.0 copy-done
  0.8 0.1 constant_dynamic-slice_fusion
  0.9 0.1 copy.15
  1.0 0.1 reshape.33
  1.1 0.2 copy.16
  1.3 0.1 reshape.34
  1.4 0.1 eq.15
  1.5 0.1 fusion.oh_hbm
  1.6 0.0 copy-start.7
  1.6 1.2 %copy.14 = bf16[12,4,6,2,2,128]{5,4,2,0,3,1:T(2,128)(2,1)S(1)} copy(bf16[12,4,6,2,2,128]{5,4,3,2,1,0:T(2,128)(2,1)} %bitcast.19) | data formatting | bytes 589824 | tf_op jit(solution)/shard_map/reshape | solution.py:428
  2.8 0.0 copy-done.3
  2.9 0.0 copy-done.7
  2.9 0.0 copy-start.1
  2.9 1.2 %copy-done.1 = bf16[2,512,512]{2,1,0:T(8,128)(2,1)S(1)} copy-done((bf16[2,512,512]{2,1,0:T(8,128)(2,1)S(1)}, bf16[2,512,512]{2,1,0:T(8,128)(2,1)}, u32[]{:S(2)}) %copy-start.1) | copy-done | bytes 1048600
  4.1 0.0 copy-start.2
  4.1 1.2 %copy-done.2 = bf16[2,512,512]{2,1,0:T(8,128)(2,1)S(1)} copy-done((bf16[2,512,512]{2,1,0:T(8,128)(2,1)S(1)}, bf16[2,512,512]{2,1,0:T(8,128)(2,1)}, u32[]{:S(2)}) %copy-start.2) | copy-done | bytes 1048600
  5.3 0.0 copy-start.4
  5.3 0.9 copy-done.4
  6.3 0.0 copy-start.5
  6.3 0.9 copy-done.5
  7.2 0.0 copy-start.6
  7.2 0.9 copy-done.6
  8.2 0.0 copy-start.8
  8.2 0.9 copy-done.8
  9.1 88.7 %swin_pair.1 = bf16[4,320,128]{2,1,0:T(8,128)(2,1)S(1)} custom-call(bf16[4,288,128]{2,1,0:T(8,128)(2,1)S(1)} %bitcast.16, bf16[2,1536,128]{2,1,0:T(8,128)(2,1)S(1)} %bitcast.17, bf16[2,128,512]{2,1,0:T(8,128)(2,1)S(1)} %copy-done.4, bf16[2,512,512]{2,1,0:T(8,128)(2,1)S(1)} %copy-done.1, bf16[2,512,512]{2,1,0:T(8,128)(2,1)S(1)} %copy-done.2, ...), custom_call_target="tpu_custom_call" | custom-call | tf_op jit(solution)/shard_map/swin_pair/pallas_call | solution.py:439
  97.8 0.8 copy.17
  (3 shorter events, 0.1 us)
Async XLA Ops:
  0.0 0.8 copy-start
  0.0 2.8 %copy-start.3 = (bf16[2,3,512,128]{3,2,1,0:T(8,128)(2,1)S(1)}, bf16[2,3,512,128]{3,2,1,0:T(8,128)(2,1)}, u32[]{:S(2)}) copy-start(bf16[2,3,512,128]{3,2,1,0:T(8,128)(2,1)} %param.12) | copy-start | bytes 2359300
  1.6 1.2 %copy-start.7 = (bf16[288,320]{1,0:T(8,128)(2,1)S(1)}, bf16[288,320]{1,0:T(8,128)(2,1)}, u32[]{:S(2)}) copy-start(bf16[288,320]{1,0:T(8,128)(2,1)} %constant.19.clone.rolled_hbm) | copy-start | bytes 552964
  2.9 1.2 %copy-start.1 = (bf16[2,512,512]{2,1,0:T(8,128)(2,1)S(1)}, bf16[2,512,512]{2,1,0:T(8,128)(2,1)}, u32[]{:S(2)}) copy-start(bf16[2,512,512]{2,1,0:T(8,128)(2,1)} %uw_ref.1) | copy-start | bytes 3145732
  4.1 1.2 %copy-start.2 = (bf16[2,512,512]{2,1,0:T(8,128)(2,1)S(1)}, bf16[2,512,512]{2,1,0:T(8,128)(2,1)}, u32[]{:S(2)}) copy-start(bf16[2,512,512]{2,1,0:T(8,128)(2,1)} %dw_ref.1) | copy-start | bytes 3145732
  5.3 0.9 copy-start.4
  6.3 0.9 copy-start.5
  7.2 0.9 copy-start.6
  8.2 0.9 copy-start.8

commit v4 on v3

--- a/solution.py
+++ b/solution.py
@@ -249,7 +249,7 @@
     def attention(b, k):
         s = source(k)
         n = nb[...]
-        query = dot(n, wq[b, s, 0:512, :]).astype(jnp.bfloat16)
+        query = (dot(n, wq[b, s, 0:512, :]) * 0.125).astype(jnp.bfloat16)
         keys = dot(n, wq[b, s, 512:1024, :]).astype(jnp.bfloat16)
         v = dot(n, wq[b, s, 1024:1536, :]).astype(jnp.bfloat16)
         for w in range(2):
@@ -261,11 +261,11 @@
                     query[rows, cols], keys[rows, cols], (((1,), (1,)), ((), ())),
                     preferred_element_type=jnp.float32,
                 )
-                scores = scores * 0.125 + bias[s * 4 + b * 2 + hh, :, 0:TOK]
+                scores = scores + bias[s * 4 + b * 2 + hh, :, 0:TOK]
                 if b == 1:
                     scores = jnp.where(same[w] > 0.5, scores, MASKED)
                 expo = jnp.exp(scores - jnp.max(scores, axis=-1, keepdims=True))
-                probs = (expo / jnp.sum(expo, axis=-1, keepdims=True)).astype(jnp.bfloat16)
+                probs = (expo * (1.0 / jnp.sum(expo, axis=-1, keepdims=True))).astype(jnp.bfloat16)
                 outs.append(dot(probs, v[rows, cols]).astype(jnp.bfloat16))
             ho[rows, :] = jnp.concatenate(outs, axis=1)
         total = dot(ho[...], wo[b, s])
@@ -291,17 +291,18 @@
     make_bias(0)
     pump(3)
     attention(0, 0)
-    pump(3)
+    pump(1)
     each_k(lambda k: pltpu.make_async_copy(tabs.at[source(k)], tabs.at[source(k)], tr_sem.at[k]).wait())
     make_bias(1)
-    pump(3)
+    pump(1)
     make_bias(2)
+    pump(1)
     make_bias(3)
     for k in range(1, 4):
         c_landed(0, 0, k)
         c_landed(0, 1, k)
         attention(0, k)
-        pump(1)
+        pump(2)
     add_total()
     renorm()
     for k in range(4):

time: 98.9 us -> 98.6 us (level)
  no operation moved by 1% of the time
where the time goes in v4:
time: 98.6 us; the launch traced here: 98.3 us
  Pallas kernels  88.3 us (90%)
  local copies, waits for them, and re-layouts  9.72 us (10%)
    pallas_call x1, Pallas kernels, local(): pl.pallas_call(functools.partial(kernel, nlon, nlat), out_shape=jax.Shape...  88.3 us
    unnamed x18, local copies, waits for them, and re-layouts  6.21 us

profile of v4, /device:TPU:0, one launch (start us, length us, event | category | flops | bytes accessed | tf_op | source)
XLA Modules:
  0.0 98.3 jit_solution(7879598365272428673)
XLA Ops:
  0.0 0.0 copy-start
  0.0 0.0 copy-start.3
  0.0 0.8 pad_bitcast_fusion
  0.8 0.0 copy-done
  0.8 0.1 constant_dynamic-slice_fusion
  0.9 0.1 copy.15
  1.0 0.1 reshape.33
  1.1 0.2 copy.16
  1.3 0.1 reshape.34
  1.4 0.1 eq.15
  1.5 0.1 fusion.oh_hbm
  1.6 0.0 copy-start.7
  1.6 1.2 %copy.14 = bf16[12,4,6,2,2,128]{5,4,2,0,3,1:T(2,128)(2,1)S(1)} copy(bf16[12,4,6,2,2,128]{5,4,3,2,1,0:T(2,128)(2,1)} %bitcast.19) | data formatting | bytes 589824 | tf_op jit(solution)/shard_map/reshape | solution.py:429
  2.8 0.0 copy-done.3
  2.9 0.0 copy-done.7
  2.9 0.0 copy-start.1
  2.9 1.2 %copy-done.1 = bf16[2,512,512]{2,1,0:T(8,128)(2,1)S(1)} copy-done((bf16[2,512,512]{2,1,0:T(8,128)(2,1)S(1)}, bf16[2,512,512]{2,1,0:T(8,128)(2,1)}, u32[]{:S(2)}) %copy-start.1) | copy-done | bytes 1048600
  4.1 0.0 copy-start.2
  4.1 1.2 %copy-done.2 = bf16[2,512,512]{2,1,0:T(8,128)(2,1)S(1)} copy-done((bf16[2,512,512]{2,1,0:T(8,128)(2,1)S(1)}, bf16[2,512,512]{2,1,0:T(8,128)(2,1)}, u32[]{:S(2)}) %copy-start.2) | copy-done | bytes 1048600
  5.3 0.0 copy-start.4
  5.3 0.9 copy-done.4
  6.3 0.0 copy-start.5
  6.3 0.9 copy-done.5
  7.2 0.0 copy-start.6
  7.2 0.9 copy-done.6
  8.2 0.0 copy-start.8
  8.2 0.9 copy-done.8
  9.1 88.3 %swin_pair.1 = bf16[4,320,128]{2,1,0:T(8,128)(2,1)S(1)} custom-call(bf16[4,288,128]{2,1,0:T(8,128)(2,1)S(1)} %bitcast.16, bf16[2,1536,128]{2,1,0:T(8,128)(2,1)S(1)} %bitcast.17, bf16[2,128,512]{2,1,0:T(8,128)(2,1)S(1)} %copy-done.4, bf16[2,512,512]{2,1,0:T(8,128)(2,1)S(1)} %copy-done.1, bf16[2,512,512]{2,1,0:T(8,128)(2,1)S(1)} %copy-done.2, ...), custom_call_target="tpu_custom_call" | custom-call | tf_op jit(solution)/shard_map/swin_pair/pallas_call | solution.py:440
  97.4 0.8 copy.17
  (3 shorter events, 0.1 us)
Async XLA Ops:
  0.0 0.8 copy-start
  0.0 2.8 %copy-start.3 = (bf16[2,3,512,128]{3,2,1,0:T(8,128)(2,1)S(1)}, bf16[2,3,512,128]{3,2,1,0:T(8,128)(2,1)}, u32[]{:S(2)}) copy-start(bf16[2,3,512,128]{3,2,1,0:T(8,128)(2,1)} %param.12) | copy-start | bytes 2359300
  1.6 1.2 %copy-start.7 = (bf16[288,320]{1,0:T(8,128)(2,1)S(1)}, bf16[288,320]{1,0:T(8,128)(2,1)}, u32[]{:S(2)}) copy-start(bf16[288,320]{1,0:T(8,128)(2,1)} %constant.19.clone.rolled_hbm) | copy-start | bytes 552964
  2.9 1.2 %copy-start.1 = (bf16[2,512,512]{2,1,0:T(8,128)(2,1)S(1)}, bf16[2,512,512]{2,1,0:T(8,128)(2,1)}, u32[]{:S(2)}) copy-start(bf16[2,512,512]{2,1,0:T(8,128)(2,1)} %uw_ref.1) | copy-start | bytes 3145732
  4.1 1.2 %copy-start.2 = (bf16[2,512,512]{2,1,0:T(8,128)(2,1)S(1)}, bf16[2,512,512]{2,1,0:T(8,128)(2,1)}, u32[]{:S(2)}) copy-start(bf16[2,512,512]{2,1,0:T(8,128)(2,1)} %dw_ref.1) | copy-start | bytes 3145732
  5.3 0.9 copy-start.4
  6.3 0.9 copy-start.5
  7.2 0.9 copy-start.6
  8.2 0.9 copy-start.8
